TPU v7x, 32 devices: a whole 2x2x4 slice. The times are simulated.
32 devices in a mesh: clip: 2 (over x), frame: 16 (over z, y, core).
Axes of the slice: x: 2, y: 2, z: 4, core: 2. Of those that a mesh axis runs over, the one named last changes fastest.
Arguments:
- feature_map: bfloat16 [32, 16320, 128], P(('clip', 'frame')), parts along dimension 0, may hold values from -4 to 4
- queries: bfloat16 [512, 128], P(('clip', 'frame')), parts along dimension 0, may hold values from -8 to 8
- corner: int32 [32, 256], P(('clip', 'frame')), parts along dimension 0, may hold values from 0 to 16198, as said below
- offsets: float32 [32, 2, 256], P(('clip', 'frame')), parts along dimension 0, may hold values from 0 to 1
- visible: int32 [32, 256], P(('clip', 'frame')), parts along dimension 0, may hold values 0 or 1
- w_embed: bfloat16 [256, 384], replicated, may hold values from -0.375 to 0.375
- w_qkv: bfloat16 [384, 1152], replicated, may hold values from -0.3125 to 0.3125
- w_out: bfloat16 [384, 384], replicated, may hold values from -0.3125 to 0.3125
- gain_attn: float32 [384], replicated, may hold values from 0.1 to 1.9
- gain_mlp: float32 [384], replicated, may hold values from 0.1 to 1.9
- w_up: bfloat16 [384, 1536], replicated, may hold values from -0.3125 to 0.3125
- w_down: bfloat16 [1536, 384], replicated, may hold values from -0.15625 to 0.15625
- w_head: bfloat16 [384, 128], replicated, may hold values from -0.3125 to 0.3125
Outputs:
- update: bfloat16 [32, 256, 128], P(('clip', 'frame')), parts along dimension 0
There are 2 independent parts, one for each index of `clip`. A program takes and returns all parts, laid end to end along the dimension named above; an argument that names none is the same for every part. Nothing has to cross between parts.
Inputs may be any that keep to these rules, and one draw needn't show every extreme that they name: `corner`: each entry is the cell index of a cell that is not in the last row or the last column of the 136 x 120 grid.
All inputs are finite; a program needn't handle non-finite values. No bound on the sum of `visible` on one device may be relied on, other than what follows from the above.
Results may differ from a plain program's by a relative error of at most 0.009.
Values may be sent and summed in bfloat16 or wider, within the bound.
A program may use at most 64 MiB of HBM per device.

v0:
```python
import math

import jax
import jax.numpy as jnp
from jax import lax
from jax.sharding import PartitionSpec as P

HEADS = 8
GRID_W = 120


def sample(frame_map, idx, frac):
    across = frac[0]
    upward = frac[1]
    weights = jnp.stack(
        [
            (1.0 - across) * (1.0 - upward),
            across * (1.0 - upward),
            (1.0 - across) * upward,
            across * upward,
        ]
    )
    places = jnp.stack([idx, idx + 1, idx + GRID_W, idx + GRID_W + 1])
    corner_rows = jnp.take(frame_map, places, axis=0).astype(jnp.float32)
    return jnp.sum(corner_rows * weights[:, :, None], axis=0).astype(jnp.bfloat16)


def correlate(frame_map, query_rows):
    count = query_rows.shape[0]
    width = query_rows.shape[1]
    block_rows = math.gcd(count, 256)
    blocks = query_rows.reshape(count // block_rows, block_rows, width)
    scale = 1.0 / math.sqrt(width)

    def single(block):
        scores = (
            lax.dot_general(
                block, frame_map, (((1,), (1,)), ((), ())), preferred_element_type=jnp.float32
            )
            * scale
        )
        probs = jax.nn.softmax(scores, axis=-1).astype(jnp.bfloat16)
        return jnp.dot(probs, frame_map, preferred_element_type=jnp.float32).astype(jnp.bfloat16)

    return lax.map(single, blocks).reshape(count, width)


def rms_scale(values, gain):
    return values * lax.rsqrt(jnp.mean(values * values, axis=-1, keepdims=True) + 1e-06) * gain


def temporal(stream, allowed, w_qkv, w_out, gain_attn, gain_mlp, w_up, w_down, w_head):
    frames = stream.shape[0]
    count = stream.shape[1]
    width = stream.shape[2]
    head_size = width // HEADS
    flowing = stream.astype(jnp.float32)
    normed = rms_scale(flowing, gain_attn).astype(jnp.bfloat16)
    packed = jnp.dot(normed, w_qkv, preferred_element_type=jnp.float32).astype(jnp.bfloat16)
    queries_h = packed[:, :, :width].reshape(frames, count, HEADS, head_size)
    keys_h = packed[:, :, width : 2 * width].reshape(frames, count, HEADS, head_size)
    values_h = packed[:, :, 2 * width :].reshape(frames, count, HEADS, head_size)
    scores = jnp.einsum(
        "fnhe,gnhe->nhfg", queries_h, keys_h, preferred_element_type=jnp.float32
    ) / math.sqrt(head_size)
    diagonal = jnp.eye(frames, dtype=bool)
    keep = jnp.logical_or(jnp.transpose(allowed)[:, None, :], diagonal[None, :, :])
    scores = jnp.where(keep[:, None, :, :], scores, jnp.float32(-1e30))
    attn = jax.nn.softmax(scores, axis=-1).astype(jnp.bfloat16)
    context = jnp.einsum("nhfg,gnhe->fnhe", attn, values_h, preferred_element_type=jnp.float32)
    context = context.astype(jnp.bfloat16).reshape(frames, count, width)
    mixed = flowing + jnp.dot(context, w_out, preferred_element_type=jnp.float32)
    normed_mlp = rms_scale(mixed, gain_mlp).astype(jnp.bfloat16)
    hidden = jax.nn.gelu(jnp.dot(normed_mlp, w_up, preferred_element_type=jnp.float32)).astype(
        jnp.bfloat16
    )
    final = (mixed + jnp.dot(hidden, w_down, preferred_element_type=jnp.float32)).astype(
        jnp.bfloat16
    )
    return jnp.dot(final, w_head, preferred_element_type=jnp.float32).astype(jnp.bfloat16)


def body(
    feature_map,
    queries,
    corner,
    offsets,
    visible,
    w_embed,
    w_qkv,
    w_out,
    gain_attn,
    gain_mlp,
    w_up,
    w_down,
    w_head,
):
    local_frames = feature_map.shape[0]
    devices = lax.axis_size("frame")
    tracks = corner.shape[1]
    per_device = tracks // devices
    sampled = jnp.stack([sample(feature_map[0], corner[0], offsets[0])])
    pooled = jnp.stack(
        [correlate(feature_map[0], lax.all_gather(queries, "frame", axis=0, tiled=True))]
    )
    token_in = jnp.concatenate([sampled, pooled], axis=-1)
    outgoing = jnp.dot(token_in, w_embed, preferred_element_type=jnp.float32).astype(jnp.bfloat16)
    outgoing = outgoing.reshape(local_frames, devices, per_device, outgoing.shape[-1])
    shown = visible.astype(jnp.bfloat16).reshape(local_frames, devices, per_device)
    stream = lax.all_to_all(outgoing, "frame", split_axis=1, concat_axis=0, tiled=True)
    seen = lax.all_to_all(shown, "frame", split_axis=1, concat_axis=0, tiled=True)
    frames = stream.shape[0]
    count = stream.shape[2]
    stream = stream.reshape(frames, count, stream.shape[3])
    seen = seen.reshape(frames, count)
    result = temporal(stream, seen > 0.5, w_qkv, w_out, gain_attn, gain_mlp, w_up, w_down, w_head)
    refined = result.reshape(frames, 1, count, result.shape[-1])
    returned = lax.all_to_all(refined, "frame", split_axis=0, concat_axis=1, tiled=True)
    return returned.reshape(local_frames, tracks, returned.shape[-1])


def solution(mesh):
    in_specs = (
        P(("clip", "frame"), None, None),
        P(("clip", "frame"), None),
        P(("clip", "frame"), None),
        P(("clip", "frame"), None, None),
        P(("clip", "frame"), None),
        P(),
        P(),
        P(),
        P(),
        P(),
        P(),
        P(),
        P(),
    )
    out_specs = P(("clip", "frame"), None, None)
    return jax.shard_map(body, mesh=mesh, in_specs=in_specs, out_specs=out_specs, check_vma=False)
```

profile of v0, /device:TPU:0, one launch (start us, length us, event | category | flops | bytes accessed | tf_op | source)
XLA Modules:
  0.0 85.4 jit_solution(4273802873749909904)
XLA Ops:
  0.0 0.0 copy-start
  0.0 0.8 convert_reduce_fusion
  0.8 0.7 reshape.361
  1.5 7.4 %all-to-all-start.1 = ((bf16[1,16,16]{2,0,1:T(2,128)(2,1)}), bf16[1,16,16]{2,0,1:T(2,128)(2,1)S(1)}, u32[]{:S(2)}, u32[]{:S(2)}) async-start(bf16[1,16,16]{2,0,1:T(2,128)(2,1)} %reshape.361), calls=%async_computation.1 | async-start | bytes 16384 | tf_op jit(solution)/shard_map/all_to_all | solution.py:111
  8.9 22.1 %all_gather.3 = bf16[256,128]{1,0:T(8,128)(2,1)S(1)} all-gather(bf16[16,128]{1,0:T(8,128)(2,1)} %param.14), channel_id=1, replica_groups=mesh['clip'=2,'frame'=16] {'frame'}, dimensions={0}, use_global_device_ids=true | all-gather | bytes 69632 | tf_op jit(solution)/shard_map/all_gather | solution.py:104
  31.0 5.1 %fusion.64 = (f32[256]{0:T(256)S(1)}, f32[256,16320]{0,1:T(8,128)S(1)}) fusion(bf16[256,128]{1,0:T(8,128)(2,1)S(1)} %all_gather.3, bf16[1,16320,128]{2,1,0:T(8,128)(2,1)} %param.13), kind=kOutput, calls=%fused_computation.94 | convolution fusion | flops 1077903104 | bytes 20956160 | tf_op jit(solution)/shard_map/while/body/eval_jaxpr/dot_general | solution.py:37
  36.1 4.4 %fusion.1 = f32[256]{0:T(256)S(1)} fusion(f32[256,16320]{0,1:T(8,128)S(1)} %get-tuple-element.31, f32[256]{0:T(256)S(1)} %get-tuple-element.30), kind=kLoop, calls=%fused_computation.5 | loop fusion | flops 8355584 | bytes 16713728 | tf_op jit(solution)/shard_map/while/body/eval_jaxpr/reduce_sum | solution.py:42
  40.5 0.0 copy-start.7
  40.5 0.0 copy-start.5
  40.5 0.0 copy-start.3
  40.5 0.0 copy-start.6
  40.5 5.6 %fusion.27 = bf16[1,256,128]{1,2,0:T(8,128)(2,1)S(1)} fusion(f32[256,16320]{0,1:T(8,128)S(1)} %get-tuple-element.31, f32[256]{0:T(256)S(1)} %fusion.1, f32[256]{0:T(256)S(1)} %get-tuple-element.30, bf16[1,16320,128]{2,1,0:T(8,128)(2,1)} %param.13), kind=kOutput, calls=%fused_computation.33 | convolution fusion | flops 1082114048 | bytes 20957184 | tf_op jit(solution)/shard_map/while/body/eval_jaxpr/dot_general | solution.py:43
  46.2 0.0 copy-done.7
  46.2 0.0 copy-start.1
  46.2 0.0 copy-done.5
  46.3 5.7 %gather_fusion = bf16[1024,128]{1,0:T(8,128)(2,1)S(1)} fusion(bf16[16320,128]{1,0:T(8,128)(2,1)} %bitcast.92, s32[1024]{0:T(1024)S(1)} %broadcast_clamp_fusion), kind=kCustom, calls=%fused_computation | custom fusion | bytes 528384 | tf_op jit(solution)/shard_map/jit(_take)/gather | solution.py:24
  52.0 0.3 multiply_reduce_fusion
  52.3 0.1 copy.35
  52.4 0.0 copy-done.3
  52.4 0.9 %convolution_convert_fusion.2 = bf16[256,384]{1,0:T(8,128)(2,1)} fusion(bf16[256,384]{1,0:T(8,128)(2,1)S(1)} %copy-done.3, bf16[1,256,128]{1,2,0:T(8,128)(2,1)S(1)} %fusion.27, bf16[1,256,128]{1,2,0:T(8,128)(2,1)S(1)} %bitcast.95), kind=kOutput, calls=%fused_computation.29 | convolution fusion | flops 50692096 | bytes 524288 | tf_op jit(solution)/shard_map/dot_general | solution.py:107
  53.4 0.0 all-to-all-done.1
  53.4 3.7 %all-to-all-start = ((bf16[1,16,16,384]{3,2,0,1:T(8,128)(2,1)}), bf16[1,16,16,384]{3,2,0,1:T(8,128)(2,1)S(1)}, u32[]{:S(2)}, u32[]{:S(2)}) async-start(bf16[1,16,16,384]{3,2,0,1:T(8,128)(2,1)} %bitcast.13), calls=%async_computation | async-start | bytes 393216 | tf_op jit(solution)/shard_map/all_to_all | solution.py:110
  57.1 0.1 copy.40
  57.2 0.1 broadcast_or_fusion
  57.3 8.6 %all-to-all-done = bf16[1,16,16,384]{3,2,0,1:T(8,128)(2,1)S(1)} async-done(((bf16[1,16,16,384]{3,2,0,1:T(8,128)(2,1)}), bf16[1,16,16,384]{3,2,0,1:T(8,128)(2,1)S(1)}, u32[]{:S(2)}, u32[]{:S(2)}) %all-to-all-start) | async-done | bytes 196640 | tf_op jit(solution)/shard_map/all_to_all | solution.py:110
  65.9 0.1 fusion.37
  66.0 0.0 copy-done.6
  66.0 0.0 copy-done.1
  66.0 0.5 convolution_convert_fusion
  66.6 0.1 fusion.63
  66.7 0.4 reshape.342
  67.1 0.4 reshape.341
  67.5 0.4 reshape.339
  68.0 2.0 %fusion.65 = (f32[16,8,16]{2,1,0:T(8,128)S(1)}, f32[16,8,16,16]{2,3,1,0:T(8,128)}) fusion(bf16[16,16,8,48]{3,2,1,0:T(8,128)(2,1)S(1)} %reshape.342, bf16[16,16,8,48]{3,2,1,0:T(8,128)(2,1)S(1)} %reshape.341, pred[16,16,16]{1,2,0:T(8,128)(4,1)S(1)} %broadcast_or_fusion), kind=kOutput, calls=%fused_computation.95 | convolution fusion | flops 3276815 | bytes 536576 | tf_op jit(solution)/shard_map/sub | solution.py:69
  70.0 0.0 copy-start.2
  70.0 0.0 copy-start.8
  70.0 1.7 %fusion.15 = bf16[16,16,8,48]{3,0,2,1:T(8,128)(2,1)S(1)} fusion(f32[16,8,16,16]{2,3,1,0:T(8,128)} %get-tuple-element.33, bf16[16,16,8,48]{3,2,1,0:T(8,128)(2,1)S(1)} %reshape.339, f32[16,8,16]{2,1,0:T(8,128)S(1)} %get-tuple-element.32), kind=kOutput, calls=%fused_computation.23 | convolution fusion | flops 3309568 | bytes 532480 | tf_op jit(solution)/shard_map/nhfg,gnhe->fnhe/dot_general | solution.py:70
  71.8 0.1 copy.45
  71.9 0.0 copy-start.4
  71.9 0.4 reshape.343
  72.3 0.0 copy-done.2
  72.3 0.4 multiply_reduce_fusion.1
  72.7 0.0 copy-done
  72.7 0.0 copy-done.8
  72.7 2.4 %fusion.20 = bf16[16,16,384]{2,1,0:T(8,128)(2,1)S(1)} fusion(f32[16,16,384]{2,1,0:T(8,128)S(1)} %get-tuple-element.35, bf16[1536,384]{1,0:T(8,128)(2,1)S(1)} %copy-done, bf16[384,1536]{1,0:T(8,128)(2,1)} %param.23, f32[384]{0:T(512)S(1)} %copy-done.8, f32[16,16]{1,0:T(8,128)S(1)} %add_rsqrt_fusion), kind=kOutput, calls=%fused_computation.28 | convolution fusion | flops 608010240 | bytes 2951680 | tf_op jit(solution)/shard_map/dot_general | solution.py:77
  75.1 0.0 copy-done.4
  75.1 0.2 fusion.26
  75.3 9.5 %all_to_all.12 = bf16[16,1,16,128]{3,2,1,0:T(8,128)(2,1)S(1)} all-to-all(bf16[16,1,16,128]{3,2,1,0:T(8,128)(2,1)S(1)} %fusion.26), channel_id=1, replica_groups=mesh['clip'=2,'frame'=16] {'frame'}, dimensions={0} | all-to-all | bytes 131072 | tf_op jit(solution)/shard_map/all_to_all | solution.py:118
  84.8 0.6 copy.60
  (10 shorter events, 0.1 us)
Async XLA Ops:
  0.0 72.7 %copy-start = (bf16[1536,384]{1,0:T(8,128)(2,1)S(1)}, bf16[1536,384]{1,0:T(8,128)(2,1)}, u32[]{:S(2)}) copy-start(bf16[1536,384]{1,0:T(8,128)(2,1)} %param.24) | copy-start | bytes 3538948
  1.5 51.9 %all-to-all-start.1 = ((bf16[1,16,16]{2,0,1:T(2,128)(2,1)}), bf16[1,16,16]{2,0,1:T(2,128)(2,1)S(1)}, u32[]{:S(2)}, u32[]{:S(2)}) async-start(bf16[1,16,16]{2,0,1:T(2,128)(2,1)} %reshape.361), calls=%async_computation.1 | async-start | bytes 16384 | tf_op jit(solution)/shard_map/all_to_all | solution.py:111
  40.5 5.7 %copy-start.7 = (f32[1,2,256]{2,1,0:T(2,128)S(1)}, f32[1,2,256]{2,1,0:T(2,128)}, u32[]{:S(2)}) copy-start(f32[1,2,256]{2,1,0:T(2,128)} %param.16) | copy-start | bytes 6148
  40.5 5.7 %copy-start.5 = (s32[1,256]{1,0:T(1,128)S(1)}, s32[1,256]{1,0:T(1,128)}, u32[]{:S(2)}) copy-start(s32[1,256]{1,0:T(1,128)} %param.15) | copy-start | bytes 3076
  40.5 11.9 %copy-start.3 = (bf16[256,384]{1,0:T(8,128)(2,1)S(1)}, bf16[256,384]{1,0:T(8,128)(2,1)}, u32[]{:S(2)}) copy-start(bf16[256,384]{1,0:T(8,128)(2,1)} %param.18) | copy-start | bytes 589828
  40.5 25.5 %copy-start.6 = (f32[384]{0:T(512)S(1)}, f32[384]{0:T(512)}, u32[]{:S(2)}) copy-start(f32[384]{0:T(512)} %param.21) | copy-start | bytes 4612
  46.2 19.9 %copy-start.1 = (bf16[384,1152]{1,0:T(8,128)(2,1)S(1)}, bf16[384,1152]{1,0:T(8,128)(2,1)}, u32[]{:S(2)}) copy-start(bf16[384,1152]{1,0:T(8,128)(2,1)} %param.19) | copy-start | bytes 2654212
  53.4 12.5 %all-to-all-start = ((bf16[1,16,16,384]{3,2,0,1:T(8,128)(2,1)}), bf16[1,16,16,384]{3,2,0,1:T(8,128)(2,1)S(1)}, u32[]{:S(2)}, u32[]{:S(2)}) async-start(bf16[1,16,16,384]{3,2,0,1:T(8,128)(2,1)} %bitcast.13), calls=%async_computation | async-start | bytes 393216 | tf_op jit(solution)/shard_map/all_to_all | solution.py:110
  70.0 2.3 %copy-start.2 = (bf16[384,384]{1,0:T(8,128)(2,1)S(1)}, bf16[384,384]{1,0:T(8,128)(2,1)}, u32[]{:S(2)}) copy-start(bf16[384,384]{1,0:T(8,128)(2,1)} %param.20) | copy-start | bytes 884740
  70.0 2.7 %copy-start.8 = (f32[384]{0:T(512)S(1)}, f32[384]{0:T(512)}, u32[]{:S(2)}) copy-start(f32[384]{0:T(512)} %param.22) | copy-start | bytes 4612
  71.9 3.2 %copy-start.4 = (bf16[384,128]{1,0:T(8,128)(2,1)S(1)}, bf16[384,128]{1,0:T(8,128)(2,1)}, u32[]{:S(2)}) copy-start(bf16[384,128]{1,0:T(8,128)(2,1)} %param.25) | copy-start | bytes 294916
where the time goes:
time: 85.8 us; the launch traced here: 85.4 us
  blocking collectives  31.6 us (37%)
  matrix products  18.9 us (22%)
  starting transfers between devices  11.1 us (13%)
  local copies, waits for them, and re-layouts  9.11 us (11%)
  waiting for transfers between devices  8.58 us (10%)
  other arithmetic  5.83 us (7%)
    all_gather x1, blocking collectives, body(): lax.all_gather(queries, 'frame', axis=0, tiled=True)  22.1 us
    all_to_all x1, blocking collectives, body(): lax.all_to_all(refined, 'frame', split_axis=0, concat_axis=1, tiled=True)  9.48 us
    all_to_all x1, waiting for transfers between devices, body(): lax.all_to_all(outgoing, 'frame', split_axis=1, concat_axis=0, tiled=True)  8.57 us
    all_to_all x1, starting transfers between devices, body(): lax.all_to_all(shown, 'frame', split_axis=1, concat_axis=0, tiled=True)  7.39 us
    gather x1, local copies, waits for them, and re-layouts, sample(): corner_rows = jnp.take(frame_map, places, axis=0).astype(jnp.float32)  5.66 us
    dot_general x1, matrix products, single(): jnp.dot(probs, frame_map, preferred_element_type=jnp.float32)  5.61 us
    dot_general x1, matrix products, single(): lax.dot_general(block, frame_map, (((1,), (1,)), ((), ())), preferred_ele...  5.11 us
    reduce_sum x1, other arithmetic, single(): probs = jax.nn.softmax(scores, axis=-1).astype(jnp.bfloat16)  4.4 us
  transfers between devices with their start and end apart: 2, of which 1 were waited for; matrix products, arithmetic and copies ran while one was open for 26% of the time, Pallas kernels for 0%

commit v1 on v0

v1 whole, which is shorter than its diff:
```python
import functools
import math

import jax
import jax.numpy as jnp
from jax import lax
from jax.experimental import pallas as pl
from jax.experimental.pallas import tpu as pltpu
from jax.sharding import PartitionSpec as P

HEADS = 8
GRID_W = 120
EPS = 1e-06
TILE = 16
WINDOW = 2 * TILE
GROUP = 8
MESH = pl.DeviceIdType.MESH
F32 = jnp.float32
BF16 = jnp.bfloat16


def pick_chunk(cells, limit):
    best = 16
    for rows in range(16, limit + 1, 16):
        if cells % rows == 0:
            best = rows
    return best


def each(count, step):
    if count == 1:
        step(0)
    else:

        def looped(i, carry):
            step(i)
            return carry

        lax.fori_loop(0, count, looped, 0)


def start_of(i, size):
    if isinstance(i, int):
        return i * size
    return pl.multiple_of(i * size, size)


def rms_scale(values, gain):
    return values * lax.rsqrt(jnp.mean(values * values, axis=-1, keepdims=True) + EPS) * gain


def dot(a, b):
    return jnp.dot(a, b, preferred_element_type=F32)


def dot_nt(a, b):
    return lax.dot_general(a, b, (((1,), (1,)), ((), ())), preferred_element_type=F32)


def dot_tn(a, b):
    return lax.dot_general(a, b, (((0,), (0,)), ((), ())), preferred_element_type=F32)


def kernel(
    n,
    fm_hbm,
    q_ref,
    tiles_s,
    corner_ref,
    off_ref,
    vis_ref,
    we_hbm,
    wqkv_hbm,
    wout_hbm,
    ga_ref,
    gm_ref,
    wup_hbm,
    wdown_hbm,
    whead_hbm,
    o_ref,
    fm,
    we,
    wqkv,
    wout,
    wup,
    wdown,
    whead,
    q_all,
    vis_all,
    table,
    tokens,
    outgoing,
    stream,
    packed,
    refined,
    returned,
    fm_sem,
    w_sem,
    q_send,
    q_recv,
    v_send,
    v_recv,
    s_send,
    s_recv,
    r_send,
    r_recv,
):
    chan = fm.shape[2]
    cells = fm.shape[0] * TILE
    tracks = q_all.shape[0]
    per = tracks // n
    rows = n * per
    width = stream.shape[1]
    me = lax.axis_index("frame")
    clip = lax.axis_index("clip")

    parts = fm_sem.shape[0]
    part_rows = fm.shape[0] // parts
    fm_copies = []
    for i in range(parts):
        piece = pl.ds(i * part_rows, part_rows)
        fm_copies.append(pltpu.make_async_copy(fm_hbm.at[piece], fm.at[piece], fm_sem.at[i]))
    for copy in fm_copies:
        copy.start()
    w_copies = [
        pltpu.make_async_copy(src, dst, w_sem.at[i])
        for i, (src, dst) in enumerate(
            [
                (we_hbm, we),
                (wqkv_hbm, wqkv),
                (wout_hbm, wout),
                (wup_hbm, wup),
                (wdown_hbm, wdown),
                (whead_hbm, whead),
            ]
        )
    ]
    for copy in w_copies:
        copy.start()

    def peer(k):
        return lax.rem(me + k, n)

    barrier = pltpu.get_barrier_semaphore()

    def greet(k, carry):
        pl.semaphore_signal(barrier, inc=1, device_id=(clip, peer(k)), device_id_type=MESH)
        return carry

    lax.fori_loop(1, n, greet, 0)
    pl.semaphore_wait(barrier, n - 1)

    mine = pl.ds(pl.multiple_of(me * per, per), per)

    def q_copy(k):
        return pltpu.make_async_remote_copy(
            src_ref=q_ref,
            dst_ref=q_all.at[mine],
            send_sem=q_send.at[k],
            recv_sem=q_recv.at[k],
            device_id=(clip, peer(k)),
            device_id_type=MESH,
        )

    def v_copy(k):
        return pltpu.make_async_remote_copy(
            src_ref=vis_ref,
            dst_ref=vis_all.at[me],
            send_sem=v_send.at[k],
            recv_sem=v_recv.at[k],
            device_id=(clip, peer(k)),
            device_id_type=MESH,
        )

    def s_copy(k):
        other = peer(k)
        return pltpu.make_async_remote_copy(
            src_ref=outgoing.at[pl.ds(pl.multiple_of(other * per, per), per)],
            dst_ref=stream.at[mine],
            send_sem=s_send.at[k],
            recv_sem=s_recv.at[k],
            device_id=(clip, other),
            device_id_type=MESH,
        )

    def r_copy(k):
        other = peer(k)
        return pltpu.make_async_remote_copy(
            src_ref=refined.at[pl.ds(pl.multiple_of(other * per, per), per)],
            dst_ref=returned.at[mine],
            send_sem=r_send.at[k],
            recv_sem=r_recv.at[k],
            device_id=(clip, other),
            device_id_type=MESH,
        )

    def over_peers(action):
        def step(k, carry):
            action(k)
            return carry

        lax.fori_loop(1, n, step, 0)

    over_peers(lambda k: q_copy(k).start())
    over_peers(lambda k: v_copy(k).start())
    q_all[mine, :] = q_ref[...]
    vis_all[me] = vis_ref[...]

    idx = corner_ref[...]
    ox = off_ref[0:1, :]
    oy = off_ref[1:2, :]
    table[...] = jnp.concatenate(
        [
            (idx % TILE).astype(F32),
            ((idx + GRID_W) % TILE + WINDOW).astype(F32),
            (1.0 - ox) * (1.0 - oy),
            ox * (1.0 - oy),
            (1.0 - ox) * oy,
            ox * oy,
            ox,
            oy,
        ],
        axis=0,
    ).T
    for copy in fm_copies:
        copy.wait()

    span = 2 * WINDOW
    lane = lax.broadcasted_iota(jnp.int32, (GROUP, GROUP * span), 1)
    own = lane // span == lax.broadcasted_iota(jnp.int32, (GROUP, GROUP * span), 0)
    within = jnp.where(own, lane % span, -2).astype(F32)

    def sample(g, carry):
        first = pl.multiple_of(g * GROUP, GROUP)
        pieces = []
        for t in range(GROUP):
            for i in range(4):
                pieces.append(fm[tiles_s[i, first + t]])
        window = jnp.concatenate(pieces, axis=0)
        facts = table[pl.ds(first, GROUP), :]
        p = facts[:, 0:1]
        r = facts[:, 1:2]
        zero = jnp.zeros_like(within)
        weight = jnp.where(within == p, facts[:, 2:3], zero)
        weight = jnp.where(within == p + 1.0, facts[:, 3:4], weight)
        weight = jnp.where(within == r, facts[:, 4:5], weight)
        weight = jnp.where(within == r + 1.0, facts[:, 5:6], weight)
        coarse = weight.astype(BF16)
        fine = (weight - coarse.astype(F32)).astype(BF16)
        both = dot(jnp.concatenate([coarse, fine], axis=0), window)
        tokens[pl.ds(first, GROUP), :] = both[:GROUP] + both[GROUP:]
        return carry

    lax.fori_loop(0, tracks // GROUP, sample, 0)

    over_peers(lambda k: q_copy(k).wait())

    block = math.gcd(tracks, 256)
    chunk = pick_chunk(cells, 1100)
    chunks = cells // chunk
    factor = math.log2(math.e) / math.sqrt(chan)
    w_copies[0].wait()

    def correlate(b):
        here = pl.ds(start_of(b, block), block)
        q = q_all[here, :]

        def piece_of(c):
            return fm[pl.ds(c * (chunk // TILE), chunk // TILE)].reshape(chunk, chan)

        def scores(c):
            return dot_nt(piece_of(c), q)

        ahead = scores(0)
        peak = total = acc = None
        for c in range(chunks):
            s = ahead
            if c + 1 < chunks:
                ahead = scores(c + 1)
            high = jnp.max(s, axis=0, keepdims=True)
            new = high if peak is None else jnp.maximum(peak, high)
            p = jnp.exp2(s * factor - new * factor)
            mass = jnp.sum(p, axis=0, keepdims=True)
            part = dot_tn(piece_of(c), p.astype(BF16))
            if peak is None:
                total, acc = mass, part
            else:
                shrink = jnp.exp2((peak - new) * factor)
                total = total * shrink + mass
                acc = acc * shrink + part
            peak = new
        pooled = (acc / total).T.astype(BF16)
        token = jnp.concatenate([tokens[here, :].astype(BF16), pooled], axis=1)
        outgoing[here, :] = dot(token, we[...]).astype(BF16)

    each(tracks // block, correlate)

    over_peers(lambda k: s_copy(k).start())
    stream[mine, :] = outgoing[mine, :]

    over_peers(lambda k: v_copy(k).wait())
    shown = vis_all[...].reshape(n, tracks).astype(F32).astype(BF16)
    tall = lax.broadcasted_iota(jnp.int32, (tracks, rows), 0)
    wide = lax.broadcasted_iota(jnp.int32, (tracks, rows), 1)
    pick = jnp.where(tall == me * per + wide % per, 1.0, 0.0).astype(BF16)
    frame_row = lax.broadcasted_iota(jnp.int32, (n, rows), 0)
    frame_col = lax.broadcasted_iota(jnp.int32, (n, rows), 1) // per
    seen = jnp.sum(
        jnp.where(frame_row == frame_col, dot(shown, pick), 0.0), axis=0, keepdims=True
    )
    for copy in w_copies[1:]:
        copy.wait()
    over_peers(lambda k: s_copy(k).wait())

    piece = math.gcd(rows, 256)

    def project(b):
        here = pl.ds(start_of(b, piece), piece)
        normed = rms_scale(stream[here, :].astype(F32), ga_ref[...]).astype(BF16)
        packed[here, :] = dot(normed, wqkv[...]).astype(BF16)

    each(rows // piece, project)

    size = width // HEADS

    def refine(b):
        first = start_of(b, piece)
        here = pl.ds(first, piece)
        q_row = lax.broadcasted_iota(jnp.int32, (piece, rows), 0) + first
        k_row = lax.broadcasted_iota(jnp.int32, (piece, rows), 1)
        same = q_row % per == k_row % per
        keep = jnp.logical_and(same, jnp.logical_or(q_row == k_row, seen > 0.5))
        bias = jnp.where(keep, 0.0, -1e30)
        tiles = [None] * (width // 128)
        for h in range(HEADS):
            lo = h * size // 128
            hi = -(-(h + 1) * size // 128)
            cols = lax.broadcasted_iota(jnp.int32, (1, (hi - lo) * 128), 1) + lo * 128
            inside = jnp.logical_and(cols >= h * size, cols < (h + 1) * size)
            gate = jnp.where(inside, 1.0, 0.0)
            qh = packed[here, lo * 128 : hi * 128] * gate.astype(BF16)
            kh = packed[:, width + lo * 128 : width + hi * 128]
            vh = packed[:, 2 * width + lo * 128 : 2 * width + hi * 128]
            s = dot_nt(qh, kh) * (1.0 / math.sqrt(size)) + bias
            p = jnp.exp(s - jnp.max(s, axis=1, keepdims=True))
            attn = (p / jnp.sum(p, axis=1, keepdims=True)).astype(BF16)
            got = dot(attn, vh) * gate
            for i in range(lo, hi):
                add = got[:, (i - lo) * 128 : (i - lo + 1) * 128]
                tiles[i] = add if tiles[i] is None else tiles[i] + add
        context = jnp.concatenate(tiles, axis=1).astype(BF16)
        mixed = stream[here, :].astype(F32) + dot(context, wout[...])
        normed = rms_scale(mixed, gm_ref[...]).astype(BF16)
        hidden = jax.nn.gelu(dot(normed, wup[...])).astype(BF16)
        final = (mixed + dot(hidden, wdown[...])).astype(BF16)
        refined[here, :] = dot(final, whead[...]).astype(BF16)

    each(rows // piece, refine)

    over_peers(lambda k: r_copy(k).start())
    returned[mine, :] = refined[mine, :]
    over_peers(lambda k: r_copy(k).wait())
    o_ref[...] = returned[...]


def body(
    feature_map,
    queries,
    corner,
    offsets,
    visible,
    w_embed,
    w_qkv,
    w_out,
    gain_attn,
    gain_mlp,
    w_up,
    w_down,
    w_head,
):
    n = lax.axis_size("frame")
    cells, chan = feature_map.shape[1:]
    tracks = corner.shape[1]
    rows = n * (tracks // n)
    width = w_embed.shape[1]
    anywhere = pl.BlockSpec(memory_space=pl.ANY)
    vmem = pl.BlockSpec(memory_space=pltpu.VMEM)
    smem = pl.BlockSpec(memory_space=pltpu.SMEM)
    dma = pltpu.SemaphoreType.DMA
    weights = [w_embed, w_qkv, w_out, w_up, w_down, w_head]
    first = corner // TILE
    second = (corner + GRID_W) // TILE
    last = cells // TILE - 1
    places = jnp.concatenate(
        [first, jnp.minimum(first + 1, last), second, jnp.minimum(second + 1, last)], axis=0
    )
    out = pl.pallas_call(
        functools.partial(kernel, n),
        out_shape=jax.ShapeDtypeStruct((tracks, chan), BF16),
        in_specs=[
            anywhere,
            vmem,
            smem,
            vmem,
            vmem,
            vmem,
            anywhere,
            anywhere,
            anywhere,
            vmem,
            vmem,
            anywhere,
            anywhere,
            anywhere,
        ],
        out_specs=vmem,
        scratch_shapes=[pltpu.VMEM((cells // TILE, TILE, chan), BF16)]
        + [pltpu.VMEM(w.shape, w.dtype) for w in weights]
        + [
            pltpu.VMEM((tracks, chan), BF16),
            pltpu.VMEM((n, 1, tracks), jnp.int32),
            pltpu.VMEM((tracks, 8), F32),
            pltpu.VMEM((tracks, chan), F32),
            pltpu.VMEM((tracks, width), BF16),
            pltpu.VMEM((rows, width), BF16),
            pltpu.VMEM((rows, w_qkv.shape[1]), BF16),
            pltpu.VMEM((rows, chan), BF16),
            pltpu.VMEM((tracks, chan), BF16),
            dma((5,)),
            dma((len(weights),)),
        ]
        + [dma((n,))] * 8,
        compiler_params=pltpu.CompilerParams(
            collective_id=0, has_side_effects=True, vmem_limit_bytes=48 * 1024 * 1024
        ),
    )(
        feature_map.reshape(cells // TILE, TILE, chan),
        queries,
        places,
        corner,
        offsets[0],
        visible,
        w_embed,
        w_qkv,
        w_out,
        gain_attn.reshape(1, width),
        gain_mlp.reshape(1, width),
        w_up,
        w_down,
        w_head,
    )
    return out[None]


def solution(mesh):
    split = ("clip", "frame")
    in_specs = (
        P(split, None, None),
        P(split, None),
        P(split, None),
        P(split, None, None),
        P(split, None),
    ) + (P(),) * 8
    out_specs = P(split, None, None)
    return jax.shard_map(body, mesh=mesh, in_specs=in_specs, out_specs=out_specs, check_vma=False)
```

time: 85.8 us -> 49 us (0.57)
  Pallas kernels: 0 us -> 36.6 us
  blocking collectives: 31.6 us -> 0 us
  matrix products: 18.9 us -> 0 us
  starting transfers between devices: 11.1 us -> 0 us
  waiting for transfers between devices: 8.58 us -> 0 us
  other arithmetic: 5.83 us -> 0.71 us
  local copies, waits for them, and re-layouts: 9.11 us -> 11.2 us
    pallas_call x0 -> x1, Pallas kernels: none -> 36.6 us  [body(): pl.pallas_call(functools.partial(kernel, n), out_shape=jax.ShapeDtypeStru...]
    all_gather x1 -> x0, blocking collectives: 22.1 us -> none  [body(): lax.all_gather(queries, 'frame', axis=0, tiled=True)]
    dot_general x8 -> x0, matrix products: 16.9 us -> none  [the longest x1 5.61 us: single(): jnp.dot(probs, frame_map, preferred_element_type=jnp.float32)]
    all_to_all x2 -> x0, starting transfers between devices: 11.1 us -> none  [the longest x1 7.39 us: body(): lax.all_to_all(shown, 'frame', split_axis=1, concat_axis=0, tiled=True)]
    all_to_all x1 -> x0, blocking collectives: 9.48 us -> none  [body(): lax.all_to_all(refined, 'frame', split_axis=0, concat_axis=1, tiled=True)]
    unnamed x19 -> x21, local copies, waits for them, and re-layouts: 0.68 us -> 9.84 us
    all_to_all x2 -> x0, waiting for transfers between devices: 8.58 us -> none  [the longest x1 8.57 us: body(): lax.all_to_all(outgoing, 'frame', split_axis=1, concat_axis=0, tiled=True)]
    gather x1 -> x0, local copies, waits for them, and re-layouts: 5.66 us -> none  [sample(): corner_rows = jnp.take(frame_map, places, axis=0).astype(jnp.float32)]
  transfers between devices with their start and end apart: 2 -> 0, of which waited for: 1 -> 0; matrix products, arithmetic and copies ran while one was open for 26% -> 0% of each run, Pallas kernels for 0% -> 0%
where the time goes in v1:
time: 49 us; the launch traced here: 48.6 us
  Pallas kernels  36.6 us (75%)
  local copies, waits for them, and re-layouts  11.2 us (23%)
  other arithmetic  0.71 us (1%)
    pallas_call x1, Pallas kernels, body(): pl.pallas_call(functools.partial(kernel, n), out_shape=jax.ShapeDtypeStru...  36.6 us
    unnamed x21, local copies, waits for them, and re-layouts  9.84 us

profile of v1, /device:TPU:0, one launch (start us, length us, event | category | flops | bytes accessed | tf_op | source)
XLA Modules:
  0.0 48.6 jit_solution(15793046624160130631)
XLA Ops:
  0.0 0.7 %reshape.10.ga_ref = f32[1,384]{1,0:T(1,128)S(1)} reshape(f32[384]{0:T(512)} %param.21) | data formatting | bytes 3072 | tf_op jit(solution)/shard_map/reshape | solution.py:446
  0.7 0.7 %reshape.11.gm_ref = f32[1,384]{1,0:T(1,128)S(1)} reshape(f32[384]{0:T(512)} %param.22) | data formatting | bytes 3072 | tf_op jit(solution)/shard_map/reshape | solution.py:447
  1.4 0.7 %add_minimum_fusion.1 = (s32[1,256]{1,0:T(1,128)S(1)}, s32[1,256]{1,0:T(1,128)S(1)}, s32[1,256]{1,0:T(1,128)S(1)}, s32[1,256]{1,0:T(1,128)S(1)}) fusion(s32[1,256]{1,0:T(1,128)} %corner_ref.1), kind=kLoop, calls=%fused_computation.10 | loop fusion | flops 8960 | bytes 5120 | tf_op jit(solution)/shard_map/min | solution.py:395
  2.1 0.0 copy-start
  2.1 1.3 %copy-done = bf16[384,1536]{1,0:T(8,128)(2,1)S(1)} copy-done((bf16[384,1536]{1,0:T(8,128)(2,1)S(1)}, bf16[384,1536]{1,0:T(8,128)(2,1)}, u32[]{:S(2)}) %copy-start) | copy-done | bytes 1179672
  3.4 0.0 copy-start.1
  3.4 1.3 %copy-done.1 = bf16[1536,384]{1,0:T(8,128)(2,1)S(1)} copy-done((bf16[1536,384]{1,0:T(8,128)(2,1)S(1)}, bf16[1536,384]{1,0:T(8,128)(2,1)}, u32[]{:S(2)}) %copy-start.1) | copy-done | bytes 1179672
  4.6 0.0 copy-start.2
  4.6 1.2 %copy-done.2 = bf16[384,1152]{1,0:T(8,128)(2,1)S(1)} copy-done((bf16[384,1152]{1,0:T(8,128)(2,1)S(1)}, bf16[384,1152]{1,0:T(8,128)(2,1)}, u32[]{:S(2)}) %copy-start.2) | copy-done | bytes 884760
  5.8 0.0 copy-start.3
  5.8 1.0 %copy-done.3 = bf16[384,384]{1,0:T(8,128)(2,1)S(1)} copy-done((bf16[384,384]{1,0:T(8,128)(2,1)S(1)}, bf16[384,384]{1,0:T(8,128)(2,1)}, u32[]{:S(2)}) %copy-start.3) | copy-done | bytes 294936
  6.8 0.0 copy-start.4
  6.8 0.9 %copy-done.4 = bf16[256,384]{1,0:T(8,128)(2,1)S(1)} copy-done((bf16[256,384]{1,0:T(8,128)(2,1)S(1)}, bf16[256,384]{1,0:T(8,128)(2,1)}, u32[]{:S(2)}) %copy-start.4) | copy-done | bytes 196632
  7.7 0.0 copy-start.5
  7.7 0.9 %copy-done.5 = bf16[384,128]{1,0:T(8,128)(2,1)S(1)} copy-done((bf16[384,128]{1,0:T(8,128)(2,1)S(1)}, bf16[384,128]{1,0:T(8,128)(2,1)}, u32[]{:S(2)}) %copy-start.5) | copy-done | bytes 98328
  8.6 0.0 copy-start.6
  8.6 0.7 %copy-done.6 = bf16[16,128]{1,0:T(8,128)(2,1)S(1)} copy-done((bf16[16,128]{1,0:T(8,128)(2,1)S(1)}, bf16[16,128]{1,0:T(8,128)(2,1)}, u32[]{:S(2)}) %copy-start.6) | copy-done | bytes 4120
  9.3 0.0 copy-start.7
  9.3 0.7 %copy-done.7 = s32[1,256]{1,0:T(1,128)S(1)} copy-done((s32[1,256]{1,0:T(1,128)S(1)}, s32[1,256]{1,0:T(1,128)}, u32[]{:S(2)}) %copy-start.7) | copy-done | bytes 1048
  9.9 0.0 copy-start.8
  9.9 0.7 %copy-done.8 = f32[1,2,256]{2,1,0:T(2,128)S(1)} copy-done((f32[1,2,256]{2,1,0:T(2,128)S(1)}, f32[1,2,256]{2,1,0:T(2,128)}, u32[]{:S(2)}) %copy-start.8) | copy-done | bytes 2072
  10.6 0.0 copy-start.9
  10.6 0.7 %copy-done.9 = s32[1,256]{1,0:T(1,128)S(1)} copy-done((s32[1,256]{1,0:T(1,128)S(1)}, s32[1,256]{1,0:T(1,128)}, u32[]{:S(2)}) %copy-start.9) | copy-done | bytes 1048
  11.3 36.6 %shard_map.127 = bf16[256,128]{1,0:T(8,128)(2,1)S(1)} custom-call(bf16[1020,16,128]{2,1,0:T(8,128)(2,1)} %bitcast.5, bf16[16,128]{1,0:T(8,128)(2,1)S(1)} %copy-done.6, s32[4,256]{1,0:T(4,128)S(1)} %pad_add_fusion.tiles_s, s32[1,256]{1,0:T(1,128)S(1)} %copy-done.7, f32[2,256]{1,0:T(2,128)S(1)} %bitcast.4, s32[1,256]{1,0:T(1,128)S(1)} %copy-done.9, ...), custom_call_target="tpu_custom_call" | custom-call | tf_op jit(solution)/shard_map/pallas_call | solution.py:397
  47.9 0.6 %copy.15 = bf16[1,256,128]{2,1,0:T(8,128)(2,1)} copy(bf16[1,256,128]{2,1,0:T(8,128)(2,1)S(1)} %bitcast.3) | data formatting | bytes 131072
  (1 shorter events, 0.0 us)
Async XLA Ops:
  2.1 1.3 %copy-start = (bf16[384,1536]{1,0:T(8,128)(2,1)S(1)}, bf16[384,1536]{1,0:T(8,128)(2,1)}, u32[]{:S(2)}) copy-start(bf16[384,1536]{1,0:T(8,128)(2,1)} %wup_hbm.1) | copy-start | bytes 3538948
  3.4 1.3 %copy-start.1 = (bf16[1536,384]{1,0:T(8,128)(2,1)S(1)}, bf16[1536,384]{1,0:T(8,128)(2,1)}, u32[]{:S(2)}) copy-start(bf16[1536,384]{1,0:T(8,128)(2,1)} %wdown_hbm.1) | copy-start | bytes 3538948
  4.6 1.2 %copy-start.2 = (bf16[384,1152]{1,0:T(8,128)(2,1)S(1)}, bf16[384,1152]{1,0:T(8,128)(2,1)}, u32[]{:S(2)}) copy-start(bf16[384,1152]{1,0:T(8,128)(2,1)} %wqkv_hbm.1) | copy-start | bytes 2654212
  5.8 1.0 %copy-start.3 = (bf16[384,384]{1,0:T(8,128)(2,1)S(1)}, bf16[384,384]{1,0:T(8,128)(2,1)}, u32[]{:S(2)}) copy-start(bf16[384,384]{1,0:T(8,128)(2,1)} %wout_hbm.1) | copy-start | bytes 884740
  6.8 0.9 %copy-start.4 = (bf16[256,384]{1,0:T(8,128)(2,1)S(1)}, bf16[256,384]{1,0:T(8,128)(2,1)}, u32[]{:S(2)}) copy-start(bf16[256,384]{1,0:T(8,128)(2,1)} %we_hbm.1) | copy-start | bytes 589828
  7.7 0.9 %copy-start.5 = (bf16[384,128]{1,0:T(8,128)(2,1)S(1)}, bf16[384,128]{1,0:T(8,128)(2,1)}, u32[]{:S(2)}) copy-start(bf16[384,128]{1,0:T(8,128)(2,1)} %whead_hbm.1) | copy-start | bytes 294916
  8.6 0.7 %copy-start.6 = (bf16[16,128]{1,0:T(8,128)(2,1)S(1)}, bf16[16,128]{1,0:T(8,128)(2,1)}, u32[]{:S(2)}) copy-start(bf16[16,128]{1,0:T(8,128)(2,1)} %q_ref.1) | copy-start | bytes 12292
  9.3 0.7 %copy-start.7 = (s32[1,256]{1,0:T(1,128)S(1)}, s32[1,256]{1,0:T(1,128)}, u32[]{:S(2)}) copy-start(s32[1,256]{1,0:T(1,128)} %corner_ref.1) | copy-start | bytes 3076
  9.9 0.7 %copy-start.8 = (f32[1,2,256]{2,1,0:T(2,128)S(1)}, f32[1,2,256]{2,1,0:T(2,128)}, u32[]{:S(2)}) copy-start(f32[1,2,256]{2,1,0:T(2,128)} %param.16) | copy-start | bytes 6148
  10.6 0.7 %copy-start.9 = (s32[1,256]{1,0:T(1,128)S(1)}, s32[1,256]{1,0:T(1,128)}, u32[]{:S(2)}) copy-start(s32[1,256]{1,0:T(1,128)} %vis_ref.1) | copy-start | bytes 3076

commit v2 on v1

--- a/solution.py
+++ b/solution.py
@@ -13,7 +13,7 @@
 EPS = 1e-06
 TILE = 16
 WINDOW = 2 * TILE
-GROUP = 8
+GROUP = 16
 MESH = pl.DeviceIdType.MESH
 F32 = jnp.float32
 BF16 = jnp.bfloat16
@@ -64,16 +64,15 @@
 def kernel(
     n,
     fm_hbm,
-    q_ref,
-    tiles_s,
-    corner_ref,
-    off_ref,
-    vis_ref,
+    q_hbm,
+    corner_hbm,
+    off_hbm,
+    vis_hbm,
     we_hbm,
     wqkv_hbm,
     wout_hbm,
-    ga_ref,
-    gm_ref,
+    ga_hbm,
+    gm_hbm,
     wup_hbm,
     wdown_hbm,
     whead_hbm,
@@ -85,21 +84,33 @@
     wup,
     wdown,
     whead,
+    ga_ref,
+    gm_ref,
+    corner_ref,
+    off_ref,
+    tiles_v,
+    tiles_s,
     q_all,
     vis_all,
     table,
-    tokens,
-    outgoing,
+    sampled,
+    sampled_in,
+    pooled,
+    pooled_in,
+    bias,
     stream,
     packed,
     refined,
     returned,
     fm_sem,
     w_sem,
+    in_sem,
     q_send,
     q_recv,
     v_send,
     v_recv,
+    a_send,
+    a_recv,
     s_send,
     s_recv,
     r_send,
@@ -114,6 +125,31 @@
     me = lax.axis_index("frame")
     clip = lax.axis_index("clip")
 
+    def peer(k):
+        return lax.rem(me + k, n)
+
+    barrier = pltpu.get_barrier_semaphore()
+
+    def greet(k, carry):
+        pl.semaphore_signal(barrier, inc=1, device_id=(clip, peer(k)), device_id_type=MESH)
+        return carry
+
+    lax.fori_loop(1, n, greet, 0)
+
+    mine = pl.ds(pl.multiple_of(me * per, per), per)
+    in_copies = [
+        pltpu.make_async_copy(src, dst, in_sem.at[i])
+        for i, (src, dst) in enumerate(
+            [
+                (q_hbm, q_all.at[mine]),
+                (vis_hbm, vis_all.at[me]),
+                (corner_hbm, corner_ref),
+                (off_hbm, off_ref),
+            ]
+        )
+    ]
+    for copy in in_copies:
+        copy.start()
     parts = fm_sem.shape[0]
     part_rows = fm.shape[0] // parts
     fm_copies = []
@@ -132,29 +168,32 @@
                 (wup_hbm, wup),
                 (wdown_hbm, wdown),
                 (whead_hbm, whead),
+                (ga_hbm, ga_ref),
+                (gm_hbm, gm_ref),
             ]
         )
     ]
-    for copy in w_copies:
-        copy.start()
-
-    def peer(k):
-        return lax.rem(me + k, n)
-
-    barrier = pltpu.get_barrier_semaphore()
-
-    def greet(k, carry):
-        pl.semaphore_signal(barrier, inc=1, device_id=(clip, peer(k)), device_id_type=MESH)
-        return carry
-
-    lax.fori_loop(1, n, greet, 0)
+    for copy in in_copies:
+        copy.wait()
+
+    idx = corner_ref[...]
+    last = fm.shape[0] - 1
+    tiles_v[...] = jnp.concatenate(
+        [
+            idx // TILE,
+            jnp.minimum(idx // TILE + 1, last),
+            (idx + GRID_W) // TILE,
+            jnp.minimum((idx + GRID_W) // TILE + 1, last),
+        ],
+        axis=0,
+    )
+    tiles_copy = pltpu.make_async_copy(tiles_v, tiles_s, in_sem.at[4])
+    tiles_copy.start()
     pl.semaphore_wait(barrier, n - 1)
-
-    mine = pl.ds(pl.multiple_of(me * per, per), per)
 
     def q_copy(k):
         return pltpu.make_async_remote_copy(
-            src_ref=q_ref,
+            src_ref=q_all.at[mine],
             dst_ref=q_all.at[mine],
             send_sem=q_send.at[k],
             recv_sem=q_recv.at[k],
@@ -164,7 +203,7 @@
 
     def v_copy(k):
         return pltpu.make_async_remote_copy(
-            src_ref=vis_ref,
+            src_ref=vis_all.at[me],
             dst_ref=vis_all.at[me],
             send_sem=v_send.at[k],
             recv_sem=v_recv.at[k],
@@ -172,27 +211,23 @@
             device_id_type=MESH,
         )
 
-    def s_copy(k):
-        other = peer(k)
-        return pltpu.make_async_remote_copy(
-            src_ref=outgoing.at[pl.ds(pl.multiple_of(other * per, per), per)],
-            dst_ref=stream.at[mine],
-            send_sem=s_send.at[k],
-            recv_sem=s_recv.at[k],
-            device_id=(clip, other),
-            device_id_type=MESH,
-        )
-
-    def r_copy(k):
-        other = peer(k)
-        return pltpu.make_async_remote_copy(
-            src_ref=refined.at[pl.ds(pl.multiple_of(other * per, per), per)],
-            dst_ref=returned.at[mine],
-            send_sem=r_send.at[k],
-            recv_sem=r_recv.at[k],
-            device_id=(clip, other),
-            device_id_type=MESH,
-        )
+    def exchange(src, dst, send, recv):
+        def copy(k):
+            other = peer(k)
+            return pltpu.make_async_remote_copy(
+                src_ref=src.at[pl.ds(pl.multiple_of(other * per, per), per)],
+                dst_ref=dst.at[mine],
+                send_sem=send.at[k],
+                recv_sem=recv.at[k],
+                device_id=(clip, other),
+                device_id_type=MESH,
+            )
+
+        return copy
+
+    a_copy = exchange(sampled, sampled_in, a_send, a_recv)
+    s_copy = exchange(pooled, pooled_in, s_send, s_recv)
+    r_copy = exchange(refined, returned, r_send, r_recv)
 
     def over_peers(action):
         def step(k, carry):
@@ -203,10 +238,7 @@
 
     over_peers(lambda k: q_copy(k).start())
     over_peers(lambda k: v_copy(k).start())
-    q_all[mine, :] = q_ref[...]
-    vis_all[me] = vis_ref[...]
-
-    idx = corner_ref[...]
+
     ox = off_ref[0:1, :]
     oy = off_ref[1:2, :]
     table[...] = jnp.concatenate(
@@ -222,8 +254,11 @@
         ],
         axis=0,
     ).T
+    tiles_copy.wait()
     for copy in fm_copies:
         copy.wait()
+    for copy in w_copies:
+        copy.start()
 
     span = 2 * WINDOW
     lane = lax.broadcasted_iota(jnp.int32, (GROUP, GROUP * span), 1)
@@ -248,10 +283,12 @@
         coarse = weight.astype(BF16)
         fine = (weight - coarse.astype(F32)).astype(BF16)
         both = dot(jnp.concatenate([coarse, fine], axis=0), window)
-        tokens[pl.ds(first, GROUP), :] = both[:GROUP] + both[GROUP:]
+        sampled[pl.ds(first, GROUP), :] = (both[:GROUP] + both[GROUP:]).astype(BF16)
         return carry
 
-    lax.fori_loop(0, tracks // GROUP, sample, 0)
+    lax.fori_loop(0, tracks // GROUP, sample, 0, unroll=2)
+    over_peers(lambda k: a_copy(k).start())
+    sampled_in[mine, :] = sampled[mine, :]
 
     over_peers(lambda k: q_copy(k).wait())
 
@@ -259,7 +296,6 @@
     chunk = pick_chunk(cells, 1100)
     chunks = cells // chunk
     factor = math.log2(math.e) / math.sqrt(chan)
-    w_copies[0].wait()
 
     def correlate(b):
         here = pl.ds(start_of(b, block), block)
@@ -289,14 +325,12 @@
                 total = total * shrink + mass
                 acc = acc * shrink + part
             peak = new
-        pooled = (acc / total).T.astype(BF16)
-        token = jnp.concatenate([tokens[here, :].astype(BF16), pooled], axis=1)
-        outgoing[here, :] = dot(token, we[...]).astype(BF16)
+        pooled[here, :] = (acc / total).T.astype(BF16)
 
     each(tracks // block, correlate)
 
     over_peers(lambda k: s_copy(k).start())
-    stream[mine, :] = outgoing[mine, :]
+    pooled_in[mine, :] = pooled[mine, :]
 
     over_peers(lambda k: v_copy(k).wait())
     shown = vis_all[...].reshape(n, tracks).astype(F32).astype(BF16)
@@ -308,29 +342,38 @@
     seen = jnp.sum(
         jnp.where(frame_row == frame_col, dot(shown, pick), 0.0), axis=0, keepdims=True
     )
-    for copy in w_copies[1:]:
-        copy.wait()
-    over_peers(lambda k: s_copy(k).wait())
-
     piece = math.gcd(rows, 256)
 
-    def project(b):
-        here = pl.ds(start_of(b, piece), piece)
-        normed = rms_scale(stream[here, :].astype(F32), ga_ref[...]).astype(BF16)
-        packed[here, :] = dot(normed, wqkv[...]).astype(BF16)
-
-    each(rows // piece, project)
-
-    size = width // HEADS
-
-    def refine(b):
+    def mask(b):
         first = start_of(b, piece)
-        here = pl.ds(first, piece)
         q_row = lax.broadcasted_iota(jnp.int32, (piece, rows), 0) + first
         k_row = lax.broadcasted_iota(jnp.int32, (piece, rows), 1)
         same = q_row % per == k_row % per
         keep = jnp.logical_and(same, jnp.logical_or(q_row == k_row, seen > 0.5))
-        bias = jnp.where(keep, 0.0, -1e30)
+        bias[pl.ds(first, piece), :] = jnp.where(keep, 0.0, -1e30)
+
+    each(rows // piece, mask)
+    for copy in w_copies:
+        copy.wait()
+    over_peers(lambda k: a_copy(k).wait())
+    over_peers(lambda k: s_copy(k).wait())
+
+    def project(b):
+        here = pl.ds(start_of(b, piece), piece)
+        token = jnp.concatenate([sampled_in[here, :], pooled_in[here, :]], axis=1)
+        embedded = dot(token, we[...]).astype(BF16)
+        stream[here, :] = embedded
+        normed = rms_scale(embedded.astype(F32), ga_ref[...][None, :]).astype(BF16)
+        packed[here, :] = dot(normed, wqkv[...]).astype(BF16)
+
+    each(rows // piece, project)
+
+    size = width // HEADS
+
+    def refine(b):
+        first = start_of(b, piece)
+        here = pl.ds(first, piece)
+        off = bias[here, :]
         tiles = [None] * (width // 128)
         for h in range(HEADS):
             lo = h * size // 128
@@ -341,7 +384,7 @@
             qh = packed[here, lo * 128 : hi * 128] * gate.astype(BF16)
             kh = packed[:, width + lo * 128 : width + hi * 128]
             vh = packed[:, 2 * width + lo * 128 : 2 * width + hi * 128]
-            s = dot_nt(qh, kh) * (1.0 / math.sqrt(size)) + bias
+            s = dot_nt(qh, kh) * (1.0 / math.sqrt(size)) + off
             p = jnp.exp(s - jnp.max(s, axis=1, keepdims=True))
             attn = (p / jnp.sum(p, axis=1, keepdims=True)).astype(BF16)
             got = dot(attn, vh) * gate
@@ -350,7 +393,7 @@
                 tiles[i] = add if tiles[i] is None else tiles[i] + add
         context = jnp.concatenate(tiles, axis=1).astype(BF16)
         mixed = stream[here, :].astype(F32) + dot(context, wout[...])
-        normed = rms_scale(mixed, gm_ref[...]).astype(BF16)
+        normed = rms_scale(mixed, gm_ref[...][None, :]).astype(BF16)
         hidden = jax.nn.gelu(dot(normed, wup[...])).astype(BF16)
         final = (mixed + dot(hidden, wdown[...])).astype(BF16)
         refined[here, :] = dot(final, whead[...]).astype(BF16)
@@ -383,68 +426,53 @@
     tracks = corner.shape[1]
     rows = n * (tracks // n)
     width = w_embed.shape[1]
-    anywhere = pl.BlockSpec(memory_space=pl.ANY)
+    hbm = pl.BlockSpec(memory_space=pltpu.HBM)
     vmem = pl.BlockSpec(memory_space=pltpu.VMEM)
-    smem = pl.BlockSpec(memory_space=pltpu.SMEM)
     dma = pltpu.SemaphoreType.DMA
-    weights = [w_embed, w_qkv, w_out, w_up, w_down, w_head]
-    first = corner // TILE
-    second = (corner + GRID_W) // TILE
-    last = cells // TILE - 1
-    places = jnp.concatenate(
-        [first, jnp.minimum(first + 1, last), second, jnp.minimum(second + 1, last)], axis=0
-    )
+    weights = [w_embed, w_qkv, w_out, w_up, w_down, w_head, gain_attn, gain_mlp]
     out = pl.pallas_call(
         functools.partial(kernel, n),
         out_shape=jax.ShapeDtypeStruct((tracks, chan), BF16),
-        in_specs=[
-            anywhere,
-            vmem,
-            smem,
-            vmem,
-            vmem,
-            vmem,
-            anywhere,
-            anywhere,
-            anywhere,
-            vmem,
-            vmem,
-            anywhere,
-            anywhere,
-            anywhere,
-        ],
+        in_specs=[hbm] * 13,
         out_specs=vmem,
         scratch_shapes=[pltpu.VMEM((cells // TILE, TILE, chan), BF16)]
         + [pltpu.VMEM(w.shape, w.dtype) for w in weights]
         + [
+            pltpu.VMEM(corner.shape, jnp.int32),
+            pltpu.VMEM(offsets.shape[1:], F32),
+            pltpu.VMEM((4, tracks), jnp.int32),
+            pltpu.SMEM((4, tracks), jnp.int32),
             pltpu.VMEM((tracks, chan), BF16),
             pltpu.VMEM((n, 1, tracks), jnp.int32),
             pltpu.VMEM((tracks, 8), F32),
-            pltpu.VMEM((tracks, chan), F32),
-            pltpu.VMEM((tracks, width), BF16),
+            pltpu.VMEM((tracks, chan), BF16),
+            pltpu.VMEM((rows, chan), BF16),
+            pltpu.VMEM((tracks, chan), BF16),
+            pltpu.VMEM((rows, chan), BF16),
+            pltpu.VMEM((rows, rows), F32),
             pltpu.VMEM((rows, width), BF16),
             pltpu.VMEM((rows, w_qkv.shape[1]), BF16),
             pltpu.VMEM((rows, chan), BF16),
             pltpu.VMEM((tracks, chan), BF16),
             dma((5,)),
             dma((len(weights),)),
+            dma((5,)),
         ]
-        + [dma((n,))] * 8,
+        + [dma((n,))] * 10,
         compiler_params=pltpu.CompilerParams(
-            collective_id=0, has_side_effects=True, vmem_limit_bytes=48 * 1024 * 1024
+            collective_id=0, has_side_effects=True, vmem_limit_bytes=60 * 1024 * 1024
         ),
     )(
         feature_map.reshape(cells // TILE, TILE, chan),
         queries,
-        places,
         corner,
         offsets[0],
         visible,
         w_embed,
         w_qkv,
         w_out,
-        gain_attn.reshape(1, width),
-        gain_mlp.reshape(1, width),
+        gain_attn,
+        gain_mlp,
         w_up,
         w_down,
         w_head,

time: 49 us -> 31.9 us (0.65)
  local copies, waits for them, and re-layouts: 11.2 us -> 1.47 us
  Pallas kernels: 36.6 us -> 30.3 us
  other arithmetic: 0.71 us -> 0 us
    unnamed x21 -> x1, local copies, waits for them, and re-layouts: 9.84 us -> 1.47 us
    pallas_call x1, Pallas kernels: 36.6 us -> 30.3 us  [body(): pl.pallas_call(functools.partial(kernel, n), out_shape=jax.ShapeDtypeStru...]
    reshape x2 -> x0, local copies, waits for them, and re-layouts: 1.37 us -> none  [the longest x1 0.68 us: body(): gain_attn.reshape(1, width)]
    min x1 -> x0, other arithmetic: 0.69 us -> none  [body(): jnp.minimum(first + 1, last)]
where the time goes in v2:
time: 31.9 us; the launch traced here: 31.8 us
  Pallas kernels  30.3 us (95%)
  local copies, waits for them, and re-layouts  1.47 us (5%)
    pallas_call x1, Pallas kernels, body(): pl.pallas_call(functools.partial(kernel, n), out_shape=jax.ShapeDtypeStru...  30.3 us
    unnamed x1, local copies, waits for them, and re-layouts  1.47 us

profile of v2, /device:TPU:0, one launch (start us, length us, event | category | flops | bytes accessed | tf_op | source)
XLA Modules:
  0.0 31.8 jit_solution(8832589373326086339)
XLA Ops:
  0.0 30.3 %shard_map.127 = bf16[256,128]{1,0:T(8,128)(2,1)} custom-call(bf16[1020,16,128]{2,1,0:T(8,128)(2,1)} %bitcast.3, bf16[16,128]{1,0:T(8,128)(2,1)} %q_hbm.1, s32[1,256]{1,0:T(1,128)} %corner_hbm.1, f32[2,256]{1,0:T(2,128)} %bitcast.5, s32[1,256]{1,0:T(1,128)} %vis_hbm.1, bf16[256,384]{1,0:T(8,128)(2,1)} %we_hbm.1, bf16[384,1152]{1,0:T(8,128)(2,1)} %wqkv_hbm.1, ...), custom_call_target="tpu_custom_call" | custom-call | tf_op jit(solution)/shard_map/pallas_call | solution.py:433
  30.3 1.5 %copy.15 = bf16[1,256,128]{2,1,0:T(8,128)(2,1)} copy(bf16[1,256,128]{2,1,0:T(8,128)(2,1)} %bitcast.4) | data formatting | bytes 131072

commit v3 on v2

--- a/solution.py
+++ b/solution.py
@@ -101,7 +101,6 @@
     stream,
     packed,
     refined,
-    returned,
     fm_sem,
     w_sem,
     in_sem,
@@ -227,14 +226,14 @@
 
     a_copy = exchange(sampled, sampled_in, a_send, a_recv)
     s_copy = exchange(pooled, pooled_in, s_send, s_recv)
-    r_copy = exchange(refined, returned, r_send, r_recv)
+    r_copy = exchange(refined, o_ref, r_send, r_recv)
 
     def over_peers(action):
         def step(k, carry):
             action(k)
             return carry
 
-        lax.fori_loop(1, n, step, 0)
+        lax.fori_loop(1, n, step, 0, unroll=5)
 
     over_peers(lambda k: q_copy(k).start())
     over_peers(lambda k: v_copy(k).start())
@@ -290,10 +289,10 @@
     over_peers(lambda k: a_copy(k).start())
     sampled_in[mine, :] = sampled[mine, :]
 
-    over_peers(lambda k: q_copy(k).wait())
+    over_peers(lambda k: q_copy(k).wait_recv())
 
     block = math.gcd(tracks, 256)
-    chunk = pick_chunk(cells, 1100)
+    chunk = pick_chunk(cells, 2720)
     chunks = cells // chunk
     factor = math.log2(math.e) / math.sqrt(chan)
 
@@ -332,7 +331,7 @@
     over_peers(lambda k: s_copy(k).start())
     pooled_in[mine, :] = pooled[mine, :]
 
-    over_peers(lambda k: v_copy(k).wait())
+    over_peers(lambda k: v_copy(k).wait_recv())
     shown = vis_all[...].reshape(n, tracks).astype(F32).astype(BF16)
     tall = lax.broadcasted_iota(jnp.int32, (tracks, rows), 0)
     wide = lax.broadcasted_iota(jnp.int32, (tracks, rows), 1)
@@ -355,8 +354,8 @@
     each(rows // piece, mask)
     for copy in w_copies:
         copy.wait()
-    over_peers(lambda k: a_copy(k).wait())
-    over_peers(lambda k: s_copy(k).wait())
+    over_peers(lambda k: a_copy(k).wait_recv())
+    over_peers(lambda k: s_copy(k).wait_recv())
 
     def project(b):
         here = pl.ds(start_of(b, piece), piece)
@@ -401,9 +400,12 @@
     each(rows // piece, refine)
 
     over_peers(lambda k: r_copy(k).start())
-    returned[mine, :] = refined[mine, :]
-    over_peers(lambda k: r_copy(k).wait())
-    o_ref[...] = returned[...]
+    kept = pltpu.make_async_copy(refined.at[mine], o_ref.at[mine], in_sem.at[5])
+    kept.start()
+    over_peers(lambda k: r_copy(k).wait_recv())
+    kept.wait()
+    for copy in (q_copy, v_copy, a_copy, s_copy, r_copy):
+        over_peers(lambda k: copy(k).wait_send())
 
 
 def body(
@@ -427,14 +429,13 @@
     rows = n * (tracks // n)
     width = w_embed.shape[1]
     hbm = pl.BlockSpec(memory_space=pltpu.HBM)
-    vmem = pl.BlockSpec(memory_space=pltpu.VMEM)
     dma = pltpu.SemaphoreType.DMA
     weights = [w_embed, w_qkv, w_out, w_up, w_down, w_head, gain_attn, gain_mlp]
     out = pl.pallas_call(
         functools.partial(kernel, n),
         out_shape=jax.ShapeDtypeStruct((tracks, chan), BF16),
         in_specs=[hbm] * 13,
-        out_specs=vmem,
+        out_specs=hbm,
         scratch_shapes=[pltpu.VMEM((cells // TILE, TILE, chan), BF16)]
         + [pltpu.VMEM(w.shape, w.dtype) for w in weights]
         + [
@@ -453,10 +454,9 @@
             pltpu.VMEM((rows, width), BF16),
             pltpu.VMEM((rows, w_qkv.shape[1]), BF16),
             pltpu.VMEM((rows, chan), BF16),
-            pltpu.VMEM((tracks, chan), BF16),
             dma((5,)),
             dma((len(weights),)),
-            dma((5,)),
+            dma((6,)),
         ]
         + [dma((n,))] * 10,
         compiler_params=pltpu.CompilerParams(

time: 31.9 us -> 30.5 us (0.956)
  Pallas kernels: 30.3 us -> 28.8 us
    pallas_call x1, Pallas kernels: 30.3 us -> 28.8 us  [body(): pl.pallas_call(functools.partial(kernel, n), out_shape=jax.ShapeDtypeStru...]
where the time goes in v3:
time: 30.5 us; the launch traced here: 30.3 us
  Pallas kernels  28.8 us (94%)
  local copies, waits for them, and re-layouts  1.47 us (5%)
    pallas_call x1, Pallas kernels, body(): pl.pallas_call(functools.partial(kernel, n), out_shape=jax.ShapeDtypeStru...  28.8 us
    unnamed x1, local copies, waits for them, and re-layouts  1.47 us

profile of v3, /device:TPU:0, one launch (start us, length us, event | category | flops | bytes accessed | tf_op | source)
XLA Modules:
  0.0 30.3 jit_solution(12806880891882260584)
XLA Ops:
  0.0 28.8 %shard_map.127 = bf16[256,128]{1,0:T(8,128)(2,1)} custom-call(bf16[1020,16,128]{2,1,0:T(8,128)(2,1)} %bitcast.3, bf16[16,128]{1,0:T(8,128)(2,1)} %q_hbm.1, s32[1,256]{1,0:T(1,128)} %corner_hbm.1, f32[2,256]{1,0:T(2,128)} %bitcast.5, s32[1,256]{1,0:T(1,128)} %vis_hbm.1, bf16[256,384]{1,0:T(8,128)(2,1)} %we_hbm.1, bf16[384,1152]{1,0:T(8,128)(2,1)} %wqkv_hbm.1, ...), custom_call_target="tpu_custom_call" | custom-call | tf_op jit(solution)/shard_map/pallas_call | solution.py:434
  28.8 1.5 %copy.15 = bf16[1,256,128]{2,1,0:T(8,128)(2,1)} copy(bf16[1,256,128]{2,1,0:T(8,128)(2,1)} %bitcast.4) | data formatting | bytes 131072
